TPU v7x, 1024 devices: a whole 4x8x16 slice. The times are simulated.
1024 devices in a mesh: dp: 64 (over x, z_lo, core), node: 16 (over y, z_hi).
Axes of the slice: x: 4, y: 8, z: 16 (z_hi: 2, z_lo: 8; z = z_hi * 8 + z_lo), core: 2. Of those that a mesh axis runs over, the one named last changes fastest.
Arguments:
- tokens: bfloat16 [16384, 12288], P('dp', 'node'), may hold values from -16 to 16
- key_weight: bfloat16 [1024, 12288], P('dp', 'node'), may hold values from -0.0546875 to 0.0546875
- key_cotangent: bfloat16 [16384, 1024], P(('dp', 'node')), may hold values from -24 to 24
Outputs:
- keys: bfloat16 [16384, 1024], P(('dp', 'node'))
- token_grad: bfloat16 [16384, 12288], P('dp', 'node')
- weight_grad: float32 [1024, 12288], P('dp', 'node')
All inputs are finite; a program needn't handle non-finite values.
Results may differ from a plain program's by a relative error of at most 0.0015.
Values may be sent and summed in bfloat16 or wider, within the bound.
A program may use at most 32 MiB of HBM per device.

v0:
```python
import jax
import jax.numpy as jnp
from jax import lax
from jax.sharding import PartitionSpec as P


def contract_last(left, right):
    return lax.dot_general(
        left, right, (((1,), (1,)), ((), ())), preferred_element_type=jnp.float32
    )


def contract_first(left, right):
    return lax.dot_general(
        left, right, (((0,), (0,)), ((), ())), preferred_element_type=jnp.float32
    )


def body(tokens, key_weight, key_cotangent):
    replicas = lax.axis_size("dp")
    second = lax.all_gather(key_weight, "dp", axis=0, tiled=True)
    keys = lax.psum_scatter(contract_last(tokens, second), "node", scatter_dimension=0, tiled=True)
    keys = keys.astype(jnp.bfloat16)
    cotangent = lax.all_gather(key_cotangent, "node", axis=0, tiled=True)
    weight_grad = (
        lax.psum_scatter(contract_first(cotangent, tokens), "dp", scatter_dimension=0, tiled=True)
        / replicas
    )
    token_grad = jnp.dot(cotangent, second, preferred_element_type=jnp.float32)
    return (keys, token_grad.astype(jnp.bfloat16), weight_grad)


def solution(mesh):
    in_specs = (P("dp", "node"), P("dp", "node"), P(("dp", "node"), None))
    out_specs = (P(("dp", "node"), None), P("dp", "node"), P("dp", "node"))
    return jax.shard_map(body, mesh=mesh, in_specs=in_specs, out_specs=out_specs, check_vma=False)
```

profile of v0, /device:TPU:24, one launch (start us, length us, event | category | flops | bytes accessed | tf_op | source)
XLA Modules:
  0.0 857.7 jit_solution(16770644854503009358)
XLA Ops:
  7.2 0.0 copy-start
  7.2 0.0 all-gather.2.cloned.1.call-start
  7.2 0.7 all-gather.2.cloned.1.call-update
  7.9 0.0 copy-start.2
  7.9 0.0 reduce-scatter.3.cloned.1.call-start
  8.0 134.3 %all-gather.2.cloned.1.call-done = bf16[1024,768]{1,0:T(8,128)(2,1)} async-done(((bf16[16,768]{1,0:T(8,128)(2,1)}), bf16[1024,768]{1,0:T(8,128)(2,1)}) %all-gather.2.cloned.1.call-update) | async-done | bytes 1572880 | tf_op jit(solution)/shard_map/all_gather | solution.py:21
  142.3 0.0 copy-done
  142.3 3.0 fusion
  145.3 0.0 reduce-scatter.3.cloned.1.call-update
  145.3 0.0 reduce-scatter.5.cloned.1.call-start
  145.4 0.0 copy-done.2
  145.4 96.6 %all_gather.7 = bf16[256,1024]{1,0:T(8,128)(2,1)S(1)} all-gather(bf16[16,1024]{1,0:T(8,128)(2,1)S(1)} %copy-done.2), channel_id=1, replica_groups=mesh['dp'=64,'node'=16] {'node'}, dimensions={0}, use_global_device_ids=true | all-gather | bytes 557056 | tf_op jit(solution)/shard_map/all_gather | solution.py:24
  242.0 2.3 fusion.1
  244.3 0.0 copy-start.1
  244.3 0.0 reduce-scatter.5.cloned.1.call-update
  244.3 1.4 copy-done.1
  245.7 1.3 convolution_convert_fusion
  247.0 163.1 %reduce-scatter.3.cloned.1.call-done = f32[16,1024]{1,0:T(8,128)} async-done(((f32[256,1024]{1,0:T(8,128)}), f32[16,1024]{1,0:T(8,128)}) %reduce-scatter.3.cloned.1.call-update) | async-done | bytes 65552 | tf_op jit(solution)/shard_map/reduce_scatter | solution.py:22
  410.1 1.5 convert_element_type.6
  411.6 438.2 %reduce-scatter.5.cloned.1.call-done = f32[16,768]{1,0:T(8,128)} async-done(((f32[1024,768]{1,0:T(8,128)}), f32[16,768]{1,0:T(8,128)}) %reduce-scatter.5.cloned.1.call-update) | async-done | bytes 49168 | tf_op jit(solution)/shard_map/reduce_scatter | solution.py:26
  849.8 1.4 broadcast_multiply_fusion
Async XLA Ops:
  7.2 135.1 %copy-start = (bf16[256,768]{1,0:T(8,128)(2,1)S(1)}, bf16[256,768]{1,0:T(8,128)(2,1)}, u32[]{:S(2)}) copy-start(bf16[256,768]{1,0:T(8,128)(2,1)} %param.3) | copy-start | bytes 1179652
  7.2 135.1 %all-gather.2.cloned.1.call-start = ((), (), s32[]{:S(2)}) async-start(), calls=%async_computation.2 | async-start | bytes 1597440 | tf_op jit(solution)/shard_map/all_gather | solution.py:21
  7.9 137.5 %copy-start.2 = (bf16[16,1024]{1,0:T(8,128)(2,1)S(1)}, bf16[16,1024]{1,0:T(8,128)(2,1)}, u32[]{:S(2)}) copy-start(bf16[16,1024]{1,0:T(8,128)(2,1)} %param.5) | copy-start | bytes 98308
  7.9 402.2 %reduce-scatter.3.cloned.1.call-start = ((), (), s32[]{:S(2)}) async-start(), calls=%async_computation.3 | async-start | bytes 1114112 | tf_op jit(solution)/shard_map/reduce_scatter | solution.py:22
  145.3 704.4 %reduce-scatter.5.cloned.1.call-start = ((), (), s32[]{:S(2)}) async-start(), calls=%async_computation.4 | async-start | bytes 3194880 | tf_op jit(solution)/shard_map/reduce_scatter | solution.py:26
  244.3 1.4 copy-start.1
Sparse Core Ops, SparseCore 0:
  10.7 131.4 all-gather.1
  147.9 262.1 reduce-scatter.2
  413.9 435.8 reduce-scatter.4
where the time goes:
time: 858 us
  waiting for transfers between devices  736 us (86%)
  blocking collectives  96.6 us (11%)
  between operations  13.8 us (2%)
    reduce_scatter x1, waiting for transfers between devices, body(): lax.psum_scatter(contract_first(cotangent, tokens), 'dp', scatter_dimensi...  438 us
    reduce_scatter x1, waiting for transfers between devices, body(): lax.psum_scatter(contract_last(tokens, second), 'node', scatter_dimension...  163 us
    all_gather x1, waiting for transfers between devices, body(): second = lax.all_gather(key_weight, 'dp', axis=0, tiled=True)  134 us
    all_gather x1, blocking collectives, body(): cotangent = lax.all_gather(key_cotangent, 'node', axis=0, tiled=True)  96.6 us
  transfers between devices with their start and end apart: 3, of which 3 were waited for; matrix products, arithmetic and copies ran while one was open for 1% of the time, Pallas kernels for 0%

commit v1 on v0

v1 whole, which is shorter than its diff:
```python
import jax
import jax.numpy as jnp
from jax import lax
from jax.experimental import pallas as pl
from jax.experimental.pallas import tpu as pltpu
from jax.sharding import PartitionSpec as P

MESH = pl.DeviceIdType.MESH
NX, NZ, NC, NY, NH = 4, 8, 2, 8, 2
D, KV, T = 768, 1024, 256
HALF = D // 2
FAR_FIRST = (4, 3, 5, 2, 6, 1, 7)

f32, bf16 = jnp.float32, jnp.bfloat16

KEY_SCALE = 2.0**11
WX_SCALE = 2.0**24
WZ_SCALE = 2.0**22


def cube(value, scale):
    value = value * scale
    return (value * value * value).astype(bf16)


def uncube(sent, scale):
    sent = sent.astype(f32)
    root = jnp.exp(jnp.log(jnp.abs(sent)) * (1.0 / 3.0)) * (1.0 / scale)
    return jnp.where(sent < 0, -root, root)


def sixth(value, scale):
    value = value * scale
    value = value * value * value
    return (value * jnp.abs(value)).astype(bf16)


def unsixth(sent, scale):
    sent = sent.astype(f32)
    root = jnp.exp(jnp.log(jnp.abs(sent)) * (1.0 / 6.0)) * (1.0 / scale)
    return jnp.where(sent < 0, -root, root)


def dot(left, right, dims):
    return lax.dot_general(left, right, (dims, ((), ())), preferred_element_type=f32)


def kernel(
    tok, wsh, csh, keys, tgrad, wgrad,
    wbuf, cown, coth, toth, wsend, wrecv, wsum, zsend, zrecv, ksend, krecv, kpart, kz, kzr, ss, rs,
):
    dp, node = lax.axis_index("dp"), lax.axis_index("node")
    x, zl, c = dp // 16, lax.rem(dp // 2, 8), lax.rem(dp, 2)
    y, zh = node // 2, lax.rem(node, 2)
    oc, oh = 1 - c, 1 - zh

    def at(px=x, pz=zl, pc=c, py=y, ph=zh):
        return ((px * NZ + pz) * NC + pc, py * NH + ph)

    def xk(k):
        return lax.rem(x + k, NX)

    def zk(k):
        return lax.rem(zl + k, NZ)

    def yk(k):
        return lax.rem(y + k, NY)

    barrier = pltpu.get_barrier_semaphore()
    peers = [at(ph=oh), at(pc=oc)]
    peers += [at(pz=zk(k)) for k in range(1, NZ)]
    peers += [at(pz=zk(k), pc=oc) for k in range(1, NZ)]
    peers += [at(py=yk(k)) for k in range(1, NY)]
    peers += [at(px=xk(k)) for k in range(1, NX)]
    for peer in peers:
        pl.semaphore_signal(barrier, inc=1, device_id=peer, device_id_type=MESH)

    cown[y, zh] = csh[...]
    wbuf[x, zl, c] = wsh[...]
    pl.semaphore_wait(barrier, len(peers))

    started = []

    def send(src, dst, peer):
        index = len(started)
        copy = pltpu.make_async_remote_copy(
            src_ref=src, dst_ref=dst, send_sem=ss.at[index], recv_sem=rs.at[index], device_id=peer, device_id_type=MESH
        )
        copy.start()
        started.append(copy)
        return copy

    def arrived(copies):
        for copy in copies:
            copy.wait_recv()

    cot_z = send(csh, cown.at[y, zh], at(ph=oh))
    cot_y = [send(csh, cown.at[y, zh], at(py=yk(k))) for k in FAR_FIRST]
    w_z = [send(wsh, wbuf.at[x, zl, c], at(pz=zk(k))) for k in FAR_FIRST]
    tok_c = send(tok.at[:, pl.ds(pl.multiple_of(oc * HALF, 128), HALF)], toth, at(pc=oc))

    arrived(cot_y)
    cot_c = [send(cown.at[:, zh], coth.at[:, zh], at(pc=oc))]
    cot_z.wait_recv()
    cot_y = [send(cown.at[y, oh], cown.at[y, oh], at(py=yk(k))) for k in FAR_FIRST]
    arrived(w_z)
    w_x = [(k, send(wbuf.at[x, :, c], wbuf.at[x, :, c], at(px=xk(k)))) for k in (2, 1, 3)]
    w_c = [(x, send(wbuf.at[x, :, c], wbuf.at[x, :, c], at(pc=oc)))]
    arrived(cot_y)
    cot_c.append(send(cown.at[:, oh], coth.at[:, oh], at(pc=oc)))

    tok_c.wait_recv()
    arrived(cot_c)
    mine = tok[:, pl.ds(pl.multiple_of(c * HALF, 128), HALF)]

    def weight_term(block):
        columns = pl.ds(pl.multiple_of(block * 256, 256), 256)
        return dot(cown[:, :, :, columns].reshape(T, 256), mine, ((0,), (0,))) + dot(
            coth[:, :, :, columns].reshape(T, 256), toth[...], ((0,), (0,))
        )

    wg_x = []
    for slot, k in enumerate((2, 1, 3)):
        wsend[slot] = cube(weight_term(xk(k)), WX_SCALE)
        wg_x.append(send(wsend.at[slot], wrecv.at[slot], at(px=xk(k))))
    own_term = weight_term(x)

    def key_block(slot, block):
        weight = wbuf[block].reshape(256, D)
        term = dot(tok[...], weight, ((1,), (1,)))
        kpart[slot] = term.reshape(NY, 32, 256)
        ksend[slot] = sixth(term, KEY_SCALE).reshape(NY, 32, 256)
        return [send(ksend.at[slot, yk(k)], krecv.at[slot, i], at(py=yk(k))) for i, k in enumerate(FAR_FIRST)]

    w_c[0][1].wait_recv()
    k_y = [key_block(0, x)]
    for k, copy in w_x:
        copy.wait_recv()
        source = xk(NX - k)
        w_c.append((source, send(wbuf.at[source, :, c], wbuf.at[source, :, c], at(pc=oc))))
    for slot in range(1, NX):
        source, copy = w_c[slot]
        copy.wait_recv()
        k_y.append(key_block(slot, source))

    arrived(wg_x)
    total = own_term
    for slot in range(3):
        total = total + uncube(wrecv[slot], WX_SCALE)
    wsum[...] = total.reshape(NZ, NC, 16, HALF)
    zsend[...] = cube(total, WZ_SCALE).reshape(NZ, NC, 16, HALF)
    wg_z = []
    for i, k in enumerate(FAR_FIRST):
        wg_z.append(send(zsend.at[zk(k), c], zrecv.at[0, i], at(pz=zk(k))))
        wg_z.append(send(zsend.at[zk(k), oc], zrecv.at[1, i], at(pz=zk(k), pc=oc)))
    wg_z.append(send(zsend.at[zl, oc], zrecv.at[1, 7], at(pc=oc)))

    grad = jnp.zeros((T, D), f32)
    for block in range(NX):
        grad = grad + dot(
            cown[:, :, :, block * 256 : (block + 1) * 256].reshape(T, 256), wbuf[block].reshape(256, D), ((1,), (0,))
        )
    tgrad[...] = grad.astype(bf16)

    k_z = []
    for slot in range(NX):
        arrived(k_y[slot])
        rows = kpart[slot, y]
        for i in range(NY - 1):
            rows = rows + unsixth(krecv[slot, i], KEY_SCALE)
        kz[slot] = rows.reshape(NH, 16, 256)
        k_z.append(send(kz.at[slot, oh], kzr.at[slot], at(ph=oh)))

    arrived(wg_z)
    for core in range(NC):
        if core == 0:
            rows = wsum[zl, c]
        else:
            rows = uncube(zrecv[1, 7], WZ_SCALE)
        for i in range(NZ - 1):
            rows = rows + uncube(zrecv[core, i], WZ_SCALE)
        half = c if core == 0 else oc
        wgrad[:, pl.ds(pl.multiple_of(half * HALF, 128), HALF)] = rows * (1.0 / 64)

    for slot in range(NX):
        k_z[slot].wait_recv()
        block = x if slot == 0 else w_c[slot][0]
        columns = pl.ds(pl.multiple_of(block * 256, 256), 256)
        keys[:, columns] = (kz[slot, zh] + kzr[slot]).astype(bf16)

    for copy in started:
        copy.wait_send()


COPIES = 1 + 7 + 7 + 1 + 1 + 7 + 3 + 1 + 1 + 3 + 7 + 3 + 21 + 15 + 4


def body(tokens, key_weight, key_cotangent):
    vmem = pl.BlockSpec(memory_space=pltpu.VMEM)
    return pl.pallas_call(
        kernel,
        out_shape=(
            jax.ShapeDtypeStruct((16, KV), bf16),
            jax.ShapeDtypeStruct((T, D), bf16),
            jax.ShapeDtypeStruct((16, D), f32),
        ),
        in_specs=[vmem] * 3,
        out_specs=(vmem,) * 3,
        scratch_shapes=[
            pltpu.VMEM((NX, NZ, NC, 16, D), bf16),
            pltpu.VMEM((NY, NH, 16, KV), bf16),
            pltpu.VMEM((NY, NH, 16, KV), bf16),
            pltpu.VMEM((T, HALF), bf16),
            pltpu.VMEM((3, T, HALF), bf16),
            pltpu.VMEM((3, T, HALF), bf16),
            pltpu.VMEM((NZ, NC, 16, HALF), f32),
            pltpu.VMEM((NZ, NC, 16, HALF), bf16),
            pltpu.VMEM((2, 8, 16, HALF), bf16),
            pltpu.VMEM((NX, NY, 32, 256), bf16),
            pltpu.VMEM((NX, NY - 1, 32, 256), bf16),
            pltpu.VMEM((NX, NY, 32, 256), f32),
            pltpu.VMEM((NX, NH, 16, 256), f32),
            pltpu.VMEM((NX, 16, 256), f32),
            pltpu.SemaphoreType.DMA((COPIES,)),
            pltpu.SemaphoreType.DMA((COPIES,)),
        ],
        compiler_params=pltpu.CompilerParams(
            collective_id=0, has_side_effects=True, vmem_limit_bytes=48 * 1024 * 1024
        ),
        name="key_projection",
    )(tokens, key_weight, key_cotangent)


def solution(mesh):
    in_specs = (P("dp", "node"), P("dp", "node"), P(("dp", "node"), None))
    out_specs = (P(("dp", "node"), None), P("dp", "node"), P("dp", "node"))
    return jax.shard_map(body, mesh=mesh, in_specs=in_specs, out_specs=out_specs, check_vma=False)
```

time: 858 us -> 76 us (0.09)
  the two profiles are of different devices: /device:TPU:24 before, /device:TPU:137 now
where the time goes in v1:
time: 76 us; the launch traced here: 75.7 us
  Pallas kernels  70.6 us (93%)
  local copies, waits for them, and re-layouts  4.47 us (6%)
    pallas_call x1, Pallas kernels, body(): pl.pallas_call(kernel, out_shape=(jax.ShapeDtypeStruct((16, KV), bf16), j...  70.6 us
    unnamed x9, local copies, waits for them, and re-layouts  4.47 us

profile of v1, /device:TPU:137, one launch (start us, length us, event | category | flops | bytes accessed | tf_op | source)
XLA Modules:
  0.0 75.7 jit_solution(9918377756701311474)
XLA Ops:
  0.6 0.0 copy-start
  0.6 1.0 %copy-done = bf16[256,768]{1,0:T(8,128)(2,1)S(1)} copy-done((bf16[256,768]{1,0:T(8,128)(2,1)S(1)}, bf16[256,768]{1,0:T(8,128)(2,1)}, u32[]{:S(2)}) %copy-start) | copy-done | bytes 393240
  1.6 0.0 copy-start.1
  1.6 0.8 copy-done.1
  2.4 0.0 copy-start.2
  2.4 0.7 copy-done.2
  3.1 70.6 %key_projection.1 = (bf16[16,1024]{1,0:T(8,128)(2,1)S(1)}, bf16[256,768]{1,0:T(8,128)(2,1)S(1)}, f32[16,768]{1,0:T(8,128)S(1)}) custom-call(bf16[256,768]{1,0:T(8,128)(2,1)S(1)} %copy-done, bf16[16,768]{1,0:T(8,128)(2,1)S(1)} %copy-done.2, bf16[16,1024]{1,0:T(8,128)(2,1)S(1)} %copy-done.1), custom_call_target="tpu_custom_call" | custom-call | tf_op jit(solution)/shard_map/key_projection/pallas_call | solution.py:200
  73.7 0.6 copy.9
  74.3 0.7 copy.10
  75.1 0.6 copy.11
Async XLA Ops:
  0.6 1.0 %copy-start = (bf16[256,768]{1,0:T(8,128)(2,1)S(1)}, bf16[256,768]{1,0:T(8,128)(2,1)}, u32[]{:S(2)}) copy-start(bf16[256,768]{1,0:T(8,128)(2,1)} %tok.1) | copy-start | bytes 1179652
  1.6 0.8 %copy-start.1 = (bf16[16,1024]{1,0:T(8,128)(2,1)S(1)}, bf16[16,1024]{1,0:T(8,128)(2,1)}, u32[]{:S(2)}) copy-start(bf16[16,1024]{1,0:T(8,128)(2,1)} %csh.1) | copy-start | bytes 98308
  2.4 0.7 copy-start.2

commit v2 on v1

v2 whole, which is shorter than its diff:
```python
import jax
import jax.numpy as jnp
from jax import lax
from jax.experimental import pallas as pl
from jax.experimental.pallas import tpu as pltpu
from jax.sharding import PartitionSpec as P

MESH = pl.DeviceIdType.MESH
NX, NZ, NC, NY, NH = 4, 8, 2, 8, 2
D, KV, T = 768, 1024, 256
HALF = D // 2
FAR_FIRST = (4, 3, 5, 2, 6, 1, 7)

f32, bf16 = jnp.float32, jnp.bfloat16

KEY_SCALE = 2.0**11
WX_SCALE = 2.0**24
WZ_SCALE = 2.0**22


def cube(value, scale):
    value = value * scale
    return (value * value * value).astype(bf16)


def uncube(sent, scale):
    sent = sent.astype(f32)
    root = jnp.exp(jnp.log(jnp.abs(sent)) * (1.0 / 3.0)) * (1.0 / scale)
    return jnp.where(sent < 0, -root, root)


def sixth(value, scale):
    value = value * scale
    value = value * value * value
    return (value * jnp.abs(value)).astype(bf16)


def unsixth(sent, scale):
    sent = sent.astype(f32)
    root = jnp.exp(jnp.log(jnp.abs(sent)) * (1.0 / 6.0)) * (1.0 / scale)
    return jnp.where(sent < 0, -root, root)


def dot(left, right, dims):
    return lax.dot_general(left, right, (dims, ((), ())), preferred_element_type=f32)


def kernel(
    tok_in, w_in, cot_in, keys, tgrad, wgrad,
    tok, wbuf, cown, coth, toth, wsend, wrecv, wsum, zsend, zrecv, ksend, krecv, kpart, ksum, kzs, kzr, ls, ss, rs,
):
    dp, node = lax.axis_index("dp"), lax.axis_index("node")
    x, zl, c = dp // 16, lax.rem(dp // 2, 8), lax.rem(dp, 2)
    y, zh = node // 2, lax.rem(node, 2)
    oc, oh = 1 - c, 1 - zh
    quad, spot = zl // 4, lax.rem(zl, 4)
    across = lax.rem(zl + 4, NZ)

    def at(px=x, pz=zl, pc=c, py=y, ph=zh):
        return ((px * NZ + pz) * NC + pc, py * NH + ph)

    def xk(k):
        return lax.rem(x + k, NX)

    def yk(k):
        return lax.rem(y + k, NY)

    def inside(k):
        return quad * 4 + lax.rem(spot + k, 4)

    def outside(k):
        return (1 - quad) * 4 + lax.rem(spot + k, 4)

    zpeers = [outside(k) for k in range(4)] + [inside(k) for k in (1, 2, 3)]
    barrier = pltpu.get_barrier_semaphore()
    peers = [at(ph=oh)]
    peers += [at(pz=pz) for pz in zpeers]
    peers += [at(pz=pz, pc=oc) for pz in zpeers]
    peers += [at(py=yk(k)) for k in FAR_FIRST]
    peers += [at(px=xk(k)) for k in (2, 1, 3)]
    peers += [at(pc=oc)]
    for peer in peers:
        pl.semaphore_signal(barrier, inc=1, device_id=peer, device_id_type=MESH)

    fetches = [
        pltpu.make_async_copy(cot_in, cown.at[y, zh], ls.at[0]),
        pltpu.make_async_copy(w_in, wbuf.at[x, zl, c], ls.at[1]),
        pltpu.make_async_copy(tok_in, tok, ls.at[2]),
    ]
    for fetch in fetches:
        fetch.start()
    for fetch in fetches:
        fetch.wait()
    pl.semaphore_wait(barrier, len(peers))

    started = []

    def send(src, dst, peer):
        index = len(started)
        copy = pltpu.make_async_remote_copy(
            src_ref=src, dst_ref=dst, send_sem=ss.at[index], recv_sem=rs.at[index], device_id=peer, device_id_type=MESH
        )
        copy.start()
        started.append(copy)
        return copy

    def same(ref, peer):
        return send(ref, ref, peer)

    def arrived(copies):
        for copy in copies:
            copy.wait_recv()

    cot_z = same(cown.at[y, zh], at(ph=oh))
    w_across = same(wbuf.at[x, zl, c], at(pz=across))
    w_z = [same(wbuf.at[x, zl, c], at(pz=inside(k))) for k in (2, 1, 3)]
    cot_y = [same(cown.at[y, zh], at(py=yk(k))) for k in FAR_FIRST]
    tok_c = send(tok.at[:, pl.ds(pl.multiple_of(oc * HALF, 128), HALF)], toth, at(pc=oc))

    def rows_of(px, group):
        which = quad if group == 0 else 1 - quad
        return wbuf.at[px, pl.ds(which * 4, 4), c]

    def spread(group):
        over_x = [(k, same(rows_of(x, group), at(px=xk(k)))) for k in (2, 1, 3)]
        return over_x, [same(rows_of(x, group), at(pc=oc))]

    def share(over_x, over_c, group):
        for k, copy in over_x:
            copy.wait_recv()
            over_c.append(same(rows_of(xk(NX - k), group), at(pc=oc)))

    def key_group(group):
        which = quad if group == 0 else 1 - quad
        weight = wbuf[:, pl.ds(which * 4, 4)].reshape(512, D)
        term = dot(tok[...], weight, ((1,), (1,)))
        kpart[group] = term.reshape(NY, 32, 512)
        ksend[group] = sixth(term, KEY_SCALE).reshape(NY, 32, 512)
        return [send(ksend.at[group, yk(k)], krecv.at[group, i], at(py=yk(k))) for i, k in enumerate(FAR_FIRST)]

    def key_sum(group, copies):
        arrived(copies)
        rows = kpart[group, y]
        for i in range(NY - 1):
            rows = rows + unsixth(krecv[group, i], KEY_SCALE)
        ksum[group] = rows.reshape(NH, 16, 512)
        kzs[group] = sixth(rows, KEY_SCALE).reshape(NH, 16, 512)
        return send(kzs.at[group, oh], kzr.at[group], at(ph=oh))

    arrived(w_z)
    x_0, c_0 = spread(0)
    arrived(cot_y)
    cot_c = [same_core(cown, coth, zh, send, at(pc=oc))]
    w_across.wait_recv()
    w_z = [same(wbuf.at[x, across, c], at(pz=inside(k))) for k in (2, 1, 3)]
    cot_z.wait_recv()
    cot_y = [same(cown.at[y, oh], at(py=yk(k))) for k in FAR_FIRST]
    share(x_0, c_0, 0)
    arrived(c_0)
    k_0 = key_group(0)
    arrived(w_z)
    x_1, c_1 = spread(1)
    arrived(cot_y)
    cot_c.append(same_core(cown, coth, oh, send, at(pc=oc)))

    tok_c.wait_recv()
    arrived(cot_c)
    mine = tok[:, pl.ds(pl.multiple_of(c * HALF, 128), HALF)]

    def weight_term(block, half):
        columns = pl.ds(pl.multiple_of(block * 256 + half * 128, 128), 128)
        return dot(cown[:, :, :, columns].reshape(T, 128), mine, ((0,), (0,))) + dot(
            coth[:, :, :, columns].reshape(T, 128), toth[...], ((0,), (0,))
        )

    g_x = []
    for part, half in enumerate((1 - quad, quad)):
        over = []
        for slot, k in enumerate((2, 1, 3)):
            wsend[part, slot] = cube(weight_term(xk(k), half), WX_SCALE)
            over.append(send(wsend.at[part, slot], wrecv.at[part, slot], at(px=xk(k))))
        g_x.append(over)
    for part, half in enumerate((1 - quad, quad)):
        wsum[part] = weight_term(x, half)

    share(x_1, c_1, 1)
    arrived(c_1)
    k_1 = key_group(1)
    k_z = [key_sum(0, k_0)]

    g_z = []
    for part in range(2):
        arrived(g_x[part])
        total = wsum[part]
        for slot in range(3):
            total = total + uncube(wrecv[part, slot], WX_SCALE)
        wsum[part] = total
        zsend[part] = cube(total, WZ_SCALE).reshape(4, NC, 16, HALF)
        for k in range(part, 4):
            pz = lax.rem(spot + k, 4)
            peer = outside(k) if part == 0 else inside(k)
            for core in range(NC):
                pc = c if core == 0 else oc
                g_z.append(send(zsend.at[part, pz, pc], zrecv.at[core, part * 4 + k], at(pz=peer, pc=pc)))
    g_z.append(send(zsend.at[1, spot, oc], zrecv.at[1, 4], at(pc=oc)))

    grad = jnp.zeros((T, D), f32)
    for block in range(NX):
        grad = grad + dot(
            cown[:, :, :, block * 256 : (block + 1) * 256].reshape(T, 256), wbuf[block].reshape(256, D), ((1,), (0,))
        )
    tgrad[...] = grad.astype(bf16)

    k_z.append(key_sum(1, k_1))

    arrived(g_z)
    first = pl.multiple_of(spot * 32 + c * 16, 16)
    for core in range(NC):
        rows = wsum[1, pl.ds(first, 16)] if core == 0 else uncube(zrecv[1, 4], WZ_SCALE)
        for slot in (0, 1, 2, 3, 5, 6, 7):
            rows = rows + uncube(zrecv[core, slot], WZ_SCALE)
        half = c if core == 0 else oc
        wgrad[:, pl.ds(pl.multiple_of(half * HALF, 128), HALF)] = rows * (1.0 / 64)

    for group in range(2):
        k_z[group].wait_recv()
        rows = (ksum[group, zh] + unsixth(kzr[group], KEY_SCALE)).astype(bf16)
        which = quad if group == 0 else 1 - quad
        for px in range(NX):
            columns = pl.ds(pl.multiple_of(px * 256 + which * 128, 128), 128)
            keys[:, columns] = rows[:, px * 128 : (px + 1) * 128]

    for copy in started:
        copy.wait_send()


def same_core(own, other, half, send, peer):
    return send(own.at[:, half], other.at[:, half], peer)


COPIES = 1 + 1 + 3 + 7 + 1 + 4 + 1 + 3 + 7 + 3 + 7 + 4 + 1 + 6 + 3 + 7 + 1 + 15 + 1


def body(tokens, key_weight, key_cotangent):
    vmem = pl.BlockSpec(memory_space=pltpu.VMEM)
    return pl.pallas_call(
        kernel,
        out_shape=(
            jax.ShapeDtypeStruct((16, KV), bf16),
            jax.ShapeDtypeStruct((T, D), bf16),
            jax.ShapeDtypeStruct((16, D), f32),
        ),
        in_specs=[pl.BlockSpec(memory_space=pltpu.HBM)] * 3,
        out_specs=(vmem,) * 3,
        scratch_shapes=[
            pltpu.VMEM((T, D), bf16),
            pltpu.VMEM((NX, NZ, NC, 16, D), bf16),
            pltpu.VMEM((NY, NH, 16, KV), bf16),
            pltpu.VMEM((NY, NH, 16, KV), bf16),
            pltpu.VMEM((T, HALF), bf16),
            pltpu.VMEM((2, 3, 128, HALF), bf16),
            pltpu.VMEM((2, 3, 128, HALF), bf16),
            pltpu.VMEM((2, 128, HALF), f32),
            pltpu.VMEM((2, 4, NC, 16, HALF), bf16),
            pltpu.VMEM((2, 8, 16, HALF), bf16),
            pltpu.VMEM((2, NY, 32, 512), bf16),
            pltpu.VMEM((2, NY - 1, 32, 512), bf16),
            pltpu.VMEM((2, NY, 32, 512), f32),
            pltpu.VMEM((2, NH, 16, 512), f32),
            pltpu.VMEM((2, NH, 16, 512), bf16),
            pltpu.VMEM((2, 16, 512), bf16),
            pltpu.SemaphoreType.DMA((3,)),
            pltpu.SemaphoreType.DMA((COPIES,)),
            pltpu.SemaphoreType.DMA((COPIES,)),
        ],
        compiler_params=pltpu.CompilerParams(
            collective_id=0, has_side_effects=True, vmem_limit_bytes=48 * 1024 * 1024
        ),
        name="key_projection",
    )(tokens, key_weight, key_cotangent)


def solution(mesh):
    in_specs = (P("dp", "node"), P("dp", "node"), P(("dp", "node"), None))
    out_specs = (P(("dp", "node"), None), P("dp", "node"), P("dp", "node"))
    return jax.shard_map(body, mesh=mesh, in_specs=in_specs, out_specs=out_specs, check_vma=False)
```

time: 76 us -> 69.1 us (0.909)
  the two profiles are of different devices: /device:TPU:137 before, /device:TPU:129 now
where the time goes in v2:
time: 69.1 us; the launch traced here: 68.8 us
  Pallas kernels  63.6 us (92%)
  local copies, waits for them, and re-layouts  4.47 us (6%)
    pallas_call x1, Pallas kernels, body(): pl.pallas_call(kernel, out_shape=(jax.ShapeDtypeStruct((16, KV), bf16), j...  63.6 us
    unnamed x9, local copies, waits for them, and re-layouts  4.47 us

profile of v2, /device:TPU:129, one launch (start us, length us, event | category | flops | bytes accessed | tf_op | source)
XLA Modules:
  0.0 68.8 jit_solution(8622396368194543976)
XLA Ops:
  0.6 0.0 copy-start
  0.6 1.0 %copy-done = bf16[256,768]{1,0:T(8,128)(2,1)S(1)} copy-done((bf16[256,768]{1,0:T(8,128)(2,1)S(1)}, bf16[256,768]{1,0:T(8,128)(2,1)}, u32[]{:S(2)}) %copy-start) | copy-done | bytes 393240
  1.6 0.0 copy-start.1
  1.6 0.8 %copy-done.1 = bf16[16,1024]{1,0:T(8,128)(2,1)S(1)} copy-done((bf16[16,1024]{1,0:T(8,128)(2,1)S(1)}, bf16[16,1024]{1,0:T(8,128)(2,1)}, u32[]{:S(2)}) %copy-start.1) | copy-done | bytes 32792
  2.4 0.0 copy-start.2
  2.4 0.7 %copy-done.2 = bf16[16,768]{1,0:T(8,128)(2,1)S(1)} copy-done((bf16[16,768]{1,0:T(8,128)(2,1)S(1)}, bf16[16,768]{1,0:T(8,128)(2,1)}, u32[]{:S(2)}) %copy-start.2) | copy-done | bytes 24600
  3.1 63.6 %key_projection.1 = (bf16[16,1024]{1,0:T(8,128)(2,1)S(1)}, bf16[256,768]{1,0:T(8,128)(2,1)S(1)}, f32[16,768]{1,0:T(8,128)S(1)}) custom-call(bf16[256,768]{1,0:T(8,128)(2,1)S(1)} %copy-done, bf16[16,768]{1,0:T(8,128)(2,1)S(1)} %copy-done.2, bf16[16,1024]{1,0:T(8,128)(2,1)S(1)} %copy-done.1), custom_call_target="tpu_custom_call" | custom-call | tf_op jit(solution)/shard_map/key_projection/pallas_call | solution.py:246
  66.8 0.6 copy.9
  67.4 0.7 %copy.10 = bf16[256,768]{1,0:T(8,128)(2,1)} copy(bf16[256,768]{1,0:T(8,128)(2,1)S(1)} %get-tuple-element.7) | data formatting | bytes 786432
  68.1 0.6 copy.11
Async XLA Ops:
  0.6 1.0 %copy-start = (bf16[256,768]{1,0:T(8,128)(2,1)S(1)}, bf16[256,768]{1,0:T(8,128)(2,1)}, u32[]{:S(2)}) copy-start(bf16[256,768]{1,0:T(8,128)(2,1)} %tok_in.1) | copy-start | bytes 1179652
  1.6 0.8 %copy-start.1 = (bf16[16,1024]{1,0:T(8,128)(2,1)S(1)}, bf16[16,1024]{1,0:T(8,128)(2,1)}, u32[]{:S(2)}) copy-start(bf16[16,1024]{1,0:T(8,128)(2,1)} %cot_in.1) | copy-start | bytes 98308
  2.4 0.7 %copy-start.2 = (bf16[16,768]{1,0:T(8,128)(2,1)S(1)}, bf16[16,768]{1,0:T(8,128)(2,1)}, u32[]{:S(2)}) copy-start(bf16[16,768]{1,0:T(8,128)(2,1)} %w_in.1) | copy-start | bytes 73732

commit v3 on v2

--- a/solution.py
+++ b/solution.py
@@ -71,12 +71,10 @@
     def outside(k):
         return (1 - quad) * 4 + lax.rem(spot + k, 4)
 
-    zpeers = [outside(k) for k in range(4)] + [inside(k) for k in (1, 2, 3)]
     barrier = pltpu.get_barrier_semaphore()
-    peers = [at(ph=oh)]
-    peers += [at(pz=pz) for pz in zpeers]
-    peers += [at(pz=pz, pc=oc) for pz in zpeers]
+    peers = [at(ph=oh), at(pz=across)]
     peers += [at(py=yk(k)) for k in FAR_FIRST]
+    peers += [at(pz=inside(k)) for k in (2, 1, 3)]
     peers += [at(px=xk(k)) for k in (2, 1, 3)]
     peers += [at(pc=oc)]
     for peer in peers:
@@ -93,6 +91,7 @@
         fetch.wait()
     pl.semaphore_wait(barrier, len(peers))
 
+
     started = []
 
     def send(src, dst, peer):
@@ -111,7 +110,7 @@
         for copy in copies:
             copy.wait_recv()
 
-    cot_z = same(cown.at[y, zh], at(ph=oh))
+    cot_z = [same(cown.at[y, zh], at(ph=oh))]
     w_across = same(wbuf.at[x, zl, c], at(pz=across))
     w_z = [same(wbuf.at[x, zl, c], at(pz=inside(k))) for k in (2, 1, 3)]
     cot_y = [same(cown.at[y, zh], at(py=yk(k))) for k in FAR_FIRST]
@@ -149,17 +148,18 @@
 
     arrived(w_z)
     x_0, c_0 = spread(0)
+    w_across.wait_recv()
+    w_z = [same(wbuf.at[x, across, c], at(pz=inside(k))) for k in (2, 1, 3)]
     arrived(cot_y)
     cot_c = [same_core(cown, coth, zh, send, at(pc=oc))]
-    w_across.wait_recv()
-    w_z = [same(wbuf.at[x, across, c], at(pz=inside(k))) for k in (2, 1, 3)]
-    cot_z.wait_recv()
+    arrived(cot_z)
     cot_y = [same(cown.at[y, oh], at(py=yk(k))) for k in FAR_FIRST]
+    arrived(w_z)
+    x_1, c_1 = spread(1)
     share(x_0, c_0, 0)
     arrived(c_0)
     k_0 = key_group(0)
-    arrived(w_z)
-    x_1, c_1 = spread(1)
+    share(x_1, c_1, 1)
     arrived(cot_y)
     cot_c.append(same_core(cown, coth, oh, send, at(pc=oc)))
 
@@ -182,10 +182,9 @@
         g_x.append(over)
     for part, half in enumerate((1 - quad, quad)):
         wsum[part] = weight_term(x, half)
-
-    share(x_1, c_1, 1)
     arrived(c_1)
     k_1 = key_group(1)
+
     k_z = [key_sum(0, k_0)]
 
     g_z = []
@@ -241,16 +240,24 @@
 COPIES = 1 + 1 + 3 + 7 + 1 + 4 + 1 + 3 + 7 + 3 + 7 + 4 + 1 + 6 + 3 + 7 + 1 + 15 + 1
 
 
+def finish(keys, tgrad, wgrad, keys_out, tgrad_out, wgrad_out):
+    tgrad_out[...] = tgrad[...]
+    keys_out[...] = keys[...]
+    wgrad_out[...] = wgrad[...]
+
+
 def body(tokens, key_weight, key_cotangent):
     vmem = pl.BlockSpec(memory_space=pltpu.VMEM)
-    return pl.pallas_call(
+    hbm = pl.BlockSpec(memory_space=pltpu.HBM)
+    shapes = (
+        jax.ShapeDtypeStruct((16, KV), bf16),
+        jax.ShapeDtypeStruct((T, D), bf16),
+        jax.ShapeDtypeStruct((16, D), f32),
+    )
+    results = pl.pallas_call(
         kernel,
-        out_shape=(
-            jax.ShapeDtypeStruct((16, KV), bf16),
-            jax.ShapeDtypeStruct((T, D), bf16),
-            jax.ShapeDtypeStruct((16, D), f32),
-        ),
-        in_specs=[pl.BlockSpec(memory_space=pltpu.HBM)] * 3,
+        out_shape=shapes,
+        in_specs=[hbm] * 3,
         out_specs=(vmem,) * 3,
         scratch_shapes=[
             pltpu.VMEM((T, D), bf16),
@@ -274,10 +281,17 @@
             pltpu.SemaphoreType.DMA((COPIES,)),
         ],
         compiler_params=pltpu.CompilerParams(
-            collective_id=0, has_side_effects=True, vmem_limit_bytes=48 * 1024 * 1024
+            collective_id=0, has_side_effects=True, vmem_limit_bytes=63 * 1024 * 1024
         ),
         name="key_projection",
     )(tokens, key_weight, key_cotangent)
+    return pl.pallas_call(
+        finish,
+        out_shape=shapes,
+        in_specs=[vmem] * 3,
+        out_specs=(vmem,) * 3,
+        name="finish",
+    )(*results)
 
 
 def solution(mesh):

time: 69.1 us -> 65.7 us (0.951)
  the two profiles are of different devices: /device:TPU:129 before, /device:TPU:16 now
where the time goes in v3:
time: 65.7 us; the launch traced here: 65.5 us
  Pallas kernels  64.9 us (99%)
    pallas_call x1, Pallas kernels, body(): pl.pallas_call(kernel, out_shape=shapes, in_specs=[hbm] * 3, out_specs=(v...  63.1 us
    pallas_call x1, Pallas kernels, body(): pl.pallas_call(finish, out_shape=shapes, in_specs=[vmem] * 3, out_specs=(...  1.78 us

profile of v3, /device:TPU:16, one launch (start us, length us, event | category | flops | bytes accessed | tf_op | source)
XLA Modules:
  0.0 65.5 jit_solution(10484210158146775508)
XLA Ops:
  0.6 63.1 %key_projection.1 = (bf16[16,1024]{1,0:T(8,128)(2,1)}, bf16[256,768]{1,0:T(8,128)(2,1)}, f32[16,768]{1,0:T(8,128)}) custom-call(bf16[256,768]{1,0:T(8,128)(2,1)} %tok_in.1, bf16[16,768]{1,0:T(8,128)(2,1)} %w_in.1, bf16[16,1024]{1,0:T(8,128)(2,1)} %cot_in.1), custom_call_target="tpu_custom_call" | custom-call | tf_op jit(solution)/shard_map/key_projection/pallas_call | solution.py:257
  63.7 1.8 %finish.1 = (bf16[16,1024]{1,0:T(8,128)(2,1)}, bf16[256,768]{1,0:T(8,128)(2,1)}, f32[16,768]{1,0:T(8,128)}) custom-call(bf16[16,1024]{1,0:T(8,128)(2,1)} %get-tuple-element.6.keys, bf16[256,768]{1,0:T(8,128)(2,1)} %get-tuple-element.7.tgrad, f32[16,768]{1,0:T(8,128)} %get-tuple-element.8.wgrad), custom_call_target="tpu_custom_call" | custom-call | tf_op jit(solution)/shard_map/finish/pallas_call | solution.py:288

commit v4 on v3

--- a/solution.py
+++ b/solution.py
@@ -77,9 +77,6 @@
     peers += [at(pz=inside(k)) for k in (2, 1, 3)]
     peers += [at(px=xk(k)) for k in (2, 1, 3)]
     peers += [at(pc=oc)]
-    for peer in peers:
-        pl.semaphore_signal(barrier, inc=1, device_id=peer, device_id_type=MESH)
-
     fetches = [
         pltpu.make_async_copy(cot_in, cown.at[y, zh], ls.at[0]),
         pltpu.make_async_copy(w_in, wbuf.at[x, zl, c], ls.at[1]),
@@ -87,8 +84,11 @@
     ]
     for fetch in fetches:
         fetch.start()
-    for fetch in fetches:
-        fetch.wait()
+    for peer in peers:
+        pl.semaphore_signal(barrier, inc=1, device_id=peer, device_id_type=MESH)
+
+    fetches[0].wait()
+    fetches[1].wait()
     pl.semaphore_wait(barrier, len(peers))
 
 
@@ -114,6 +114,7 @@
     w_across = same(wbuf.at[x, zl, c], at(pz=across))
     w_z = [same(wbuf.at[x, zl, c], at(pz=inside(k))) for k in (2, 1, 3)]
     cot_y = [same(cown.at[y, zh], at(py=yk(k))) for k in FAR_FIRST]
+    fetches[2].wait()
     tok_c = send(tok.at[:, pl.ds(pl.multiple_of(oc * HALF, 128), HALF)], toth, at(pc=oc))
 
     def rows_of(px, group):

time: 65.7 us -> 65.7 us (level)
  no operation moved by 1% of the time
where the time goes in v4:
time: 65.7 us; the launch traced here: 65.5 us
  Pallas kernels  64.9 us (99%)
    pallas_call x1, Pallas kernels, body(): pl.pallas_call(kernel, out_shape=shapes, in_specs=[hbm] * 3, out_specs=(v...  63.1 us
    pallas_call x1, Pallas kernels, body(): pl.pallas_call(finish, out_shape=shapes, in_specs=[vmem] * 3, out_specs=(...  1.78 us

profile of v4, /device:TPU:16, one launch (start us, length us, event | category | flops | bytes accessed | tf_op | source)
XLA Modules:
  0.0 65.5 jit_solution(14195655394482130060)
XLA Ops:
  0.6 63.1 %key_projection.1 = (bf16[16,1024]{1,0:T(8,128)(2,1)}, bf16[256,768]{1,0:T(8,128)(2,1)}, f32[16,768]{1,0:T(8,128)}) custom-call(bf16[256,768]{1,0:T(8,128)(2,1)} %tok_in.1, bf16[16,768]{1,0:T(8,128)(2,1)} %w_in.1, bf16[16,1024]{1,0:T(8,128)(2,1)} %cot_in.1), custom_call_target="tpu_custom_call" | custom-call | tf_op jit(solution)/shard_map/key_projection/pallas_call | solution.py:258
  63.8 1.8 %finish.1 = (bf16[16,1024]{1,0:T(8,128)(2,1)}, bf16[256,768]{1,0:T(8,128)(2,1)}, f32[16,768]{1,0:T(8,128)}) custom-call(bf16[16,1024]{1,0:T(8,128)(2,1)} %get-tuple-element.6.keys, bf16[256,768]{1,0:T(8,128)(2,1)} %get-tuple-element.7.tgrad, f32[16,768]{1,0:T(8,128)} %get-tuple-element.8.wgrad), custom_call_target="tpu_custom_call" | custom-call | tf_op jit(solution)/shard_map/finish/pallas_call | solution.py:289
